TPU v7x, 32 devices: a whole 2x2x4 slice. The times are simulated.
32 devices in a mesh: row: 8 (over z, x), col: 4 (over y, core).
Axes of the slice: x: 2, y: 2, z: 4, core: 2. Of those that a mesh axis runs over, the one named last changes fastest.
Arguments:
- eigvecs: float32 [2048, 65536], P(('col', 'row')), may hold values from -6 to 6
- reflectors: float32 [4, 256, 65536], P(None, 'col', 'row'), may hold values from -0.0234375 to 0.0234375
- tfactors: float32 [4, 256, 256], replicated, may hold values from -0.5 to 2, as said below
Outputs:
- backed: float32 [65536, 2048], P('row', 'col')
Inputs may be any that keep to these rules, and one draw needn't show every extreme that they name: `tfactors`: each block's factor is upper triangular with diagonal entries between 1 and 2.
All inputs are finite; a program needn't handle non-finite values.
Results may differ from a plain program's by a relative error of at most 0.0001.
Values sent between devices are 32-bit elements; how exact they have to be, the bound alone decides.
A program may use at most 128 MiB of HBM per device.

v0:
```python
import jax
import jax.numpy as jnp
from jax import lax
from jax.sharding import PartitionSpec as P


def matmul(left, right):
    return jnp.dot(left, right, precision=lax.Precision.HIGHEST, preferred_element_type=jnp.float32)


def inner_rows(left, right):
    return lax.dot_general(
        left,
        right,
        (((0,), (0,)), ((), ())),
        precision=lax.Precision.HIGHEST,
        preferred_element_type=jnp.float32,
    )


def body(eigvecs, reflectors, tfactors):
    arrived = lax.all_to_all(eigvecs, "row", split_axis=1, concat_axis=0, tiled=True)
    current = arrived.T
    blocks = tfactors.shape[0]
    for block in range(blocks - 1, -1, -1):
        vectors = lax.all_gather(reflectors[block], "col", axis=0, tiled=True)
        inner_part = matmul(vectors, current)
        inner_sum = lax.psum(inner_part, "row")
        scaled = matmul(tfactors[block], inner_sum)
        current = current - inner_rows(vectors, scaled)
    return current


def solution(mesh):
    in_specs = (P(("col", "row"), None), P(None, "col", "row"), P())
    out_specs = P("row", "col")
    return jax.shard_map(body, mesh=mesh, in_specs=in_specs, out_specs=out_specs, check_vma=False)
```

profile of v0, /device:TPU:0, one launch (start us, length us, event | category | flops | bytes accessed | tf_op | source)
XLA Modules:
  0.0 982.3 jit_solution(12616680192022693570)
XLA Ops:
  6.5 11.7 %copy.8 = f32[8,8,8,8192]{3,2,0,1:T(8,128)} copy(f32[8,8,8,8192]{3,2,1,0:T(8,128)} %bitcast.66) | data formatting | bytes 33554432 | tf_op jit(solution)/shard_map/all_to_all | solution.py:22
  18.2 7.3 all-to-all-start
  25.5 0.0 all-gather.9.cloned.1.call-start
  25.5 6.9 fusion.33
  32.4 0.0 all-gather.9.cloned.1.call-update
  32.4 0.0 all-reduce.5.cloned.1.call-start
  32.5 59.8 %all-gather.9.cloned.1.call-done = f32[1,256,8192]{2,1,0:T(8,128)} async-done(((f32[1,64,8192]{2,1,0:T(8,128)}), f32[1,256,8192]{2,1,0:T(8,128)}) %all-gather.9.cloned.1.call-update) | async-done | bytes 8388624 | tf_op jit(solution)/shard_map/all_gather | solution.py:26
  92.3 296.3 %all-to-all-done = f32[64,8,8192]{2,0,1:T(8,128)} async-done(((f32[64,8,8192]{2,0,1:T(8,128)}), f32[64,8,8192]{2,0,1:T(8,128)}, u32[]{:S(2)}, u32[]{:S(2)}) %all-to-all-start) | async-done | bytes 16777248 | tf_op jit(solution)/shard_map/all_to_all | solution.py:22
  388.5 0.0 copy-start
  388.5 19.4 %fusion.10 = f32[256,512]{1,0:T(8,128)} fusion(f32[512,8192]{1,0:T(8,128)} %bitcast.1, f32[1,256,8192]{2,1,0:T(8,128)} %all-gather.9.cloned.1.call-done), kind=kOutput, calls=%fused_computation.15 | convolution fusion | flops 12884901888 | bytes 25690112 | tf_op jit(solution)/shard_map/dot_general | solution.py:8
  408.0 0.0 all-reduce.5.cloned.1.call-update
  408.0 0.0 all-gather.11.cloned.1.call-start
  408.1 0.7 all-gather.11.cloned.1.call-update
  408.7 0.6 all-reduce.7.cloned.1.call-start
  409.3 70.2 %all-reduce.5.cloned.1.call-done = f32[256,512]{1,0:T(8,128)} async-done(((f32[256,512]{1,0:T(8,128)}), f32[256,512]{1,0:T(8,128)}) %all-reduce.5.cloned.1.call-update) | async-done | bytes 524304 | tf_op jit(solution)/shard_map/psum | solution.py:28
  479.6 0.0 copy-done
  479.6 2.0 fusion.27
  481.6 25.9 %convolution_subtract_fusion.2 = f32[512,8192]{1,0:T(8,128)} fusion(f32[512,8192]{1,0:T(8,128)} %bitcast.1, f32[512,256]{1,0:T(8,128)S(1)} %fusion.27, f32[1,256,8192]{2,1,0:T(8,128)} %all-gather.9.cloned.1.call-done), kind=kOutput, calls=%fused_computation.4 | convolution fusion | flops 12889096192 | bytes 42467328 | tf_op jit(solution)/shard_map/dot_general | solution.py:12
  507.5 31.3 %all-gather.11.cloned.1.call-done = f32[1,256,8192]{2,1,0:T(8,128)} async-done(((f32[1,64,8192]{2,1,0:T(8,128)}), f32[1,256,8192]{2,1,0:T(8,128)}) %all-gather.11.cloned.1.call-update) | async-done | bytes 8388624 | tf_op jit(solution)/shard_map/all_gather | solution.py:26
  538.8 18.4 %fusion.12 = f32[256,512]{0,1:T(8,128)} fusion(f32[512,8192]{1,0:T(8,128)} %convolution_subtract_fusion.2, f32[1,256,8192]{2,1,0:T(8,128)} %all-gather.11.cloned.1.call-done), kind=kOutput, calls=%fused_computation.17 | convolution fusion | flops 12884901888 | bytes 25690112 | tf_op jit(solution)/shard_map/dot_general | solution.py:8
  557.2 0.0 all-reduce.7.cloned.1.call-update
  557.3 0.0 all-gather.13.cloned.1.call-start
  557.3 0.5 all-gather.13.cloned.1.call-update
  557.8 0.2 all-reduce.9.cloned.1.call-start
  558.1 71.7 %all-reduce.7.cloned.1.call-done = f32[256,512]{0,1:T(8,128)} async-done(((f32[256,512]{0,1:T(8,128)}), f32[256,512]{0,1:T(8,128)}) %all-reduce.7.cloned.1.call-update) | async-done | bytes 524304 | tf_op jit(solution)/shard_map/psum | solution.py:28
  629.8 1.7 fusion.25
  631.5 25.9 %convolution_subtract_fusion.1 = f32[512,8192]{1,0:T(8,128)} fusion(f32[512,8192]{1,0:T(8,128)} %convolution_subtract_fusion.2, f32[512,256]{1,0:T(8,128)S(1)} %fusion.25, f32[1,256,8192]{2,1,0:T(8,128)} %all-gather.11.cloned.1.call-done), kind=kOutput, calls=%fused_computation.3 | convolution fusion | flops 12889096192 | bytes 42467328 | tf_op jit(solution)/shard_map/dot_general | solution.py:12
  657.4 31.4 %all-gather.13.cloned.1.call-done = f32[1,256,8192]{2,1,0:T(8,128)} async-done(((f32[1,64,8192]{2,1,0:T(8,128)}), f32[1,256,8192]{2,1,0:T(8,128)}) %all-gather.13.cloned.1.call-update) | async-done | bytes 8388624 | tf_op jit(solution)/shard_map/all_gather | solution.py:26
  688.8 18.4 %fusion.15 = f32[256,512]{0,1:T(8,128)} fusion(f32[512,8192]{1,0:T(8,128)} %convolution_subtract_fusion.1, f32[1,256,8192]{2,1,0:T(8,128)} %all-gather.13.cloned.1.call-done), kind=kOutput, calls=%fused_computation.18 | convolution fusion | flops 12884901888 | bytes 25690112 | tf_op jit(solution)/shard_map/dot_general | solution.py:8
  707.2 0.0 all-reduce.9.cloned.1.call-update
  707.3 0.0 all-gather.15.cloned.1.call-start
  707.3 0.7 all-gather.15.cloned.1.call-update
  708.0 0.3 all-reduce.11.cloned.1.call-start
  708.3 71.5 %all-reduce.9.cloned.1.call-done = f32[256,512]{0,1:T(8,128)} async-done(((f32[256,512]{0,1:T(8,128)}), f32[256,512]{0,1:T(8,128)}) %all-reduce.9.cloned.1.call-update) | async-done | bytes 524304 | tf_op jit(solution)/shard_map/psum | solution.py:28
  779.8 1.7 fusion.23
  781.5 25.9 %convolution_subtract_fusion = f32[512,8192]{1,0:T(8,128)} fusion(f32[512,8192]{1,0:T(8,128)} %convolution_subtract_fusion.1, f32[512,256]{1,0:T(8,128)S(1)} %fusion.23, f32[1,256,8192]{2,1,0:T(8,128)} %all-gather.13.cloned.1.call-done), kind=kOutput, calls=%fused_computation.2 | convolution fusion | flops 12889096192 | bytes 42467328 | tf_op jit(solution)/shard_map/dot_general | solution.py:12
  807.4 31.7 %all-gather.15.cloned.1.call-done = f32[1,256,8192]{2,1,0:T(8,128)} async-done(((f32[1,64,8192]{2,1,0:T(8,128)}), f32[1,256,8192]{2,1,0:T(8,128)}) %all-gather.15.cloned.1.call-update) | async-done | bytes 8388624 | tf_op jit(solution)/shard_map/all_gather | solution.py:26
  839.0 18.4 %fusion.18 = f32[256,512]{0,1:T(8,128)} fusion(f32[512,8192]{1,0:T(8,128)} %convolution_subtract_fusion, f32[1,256,8192]{2,1,0:T(8,128)} %all-gather.15.cloned.1.call-done), kind=kOutput, calls=%fused_computation.19 | convolution fusion | flops 12884901888 | bytes 25690112 | tf_op jit(solution)/shard_map/dot_general | solution.py:8
  857.4 0.0 all-reduce.11.cloned.1.call-update
  857.5 72.5 %all-reduce.11.cloned.1.call-done = f32[256,512]{0,1:T(8,128)} async-done(((f32[256,512]{0,1:T(8,128)}), f32[256,512]{0,1:T(8,128)}) %all-reduce.11.cloned.1.call-update) | async-done | bytes 524304 | tf_op jit(solution)/shard_map/psum | solution.py:28
  930.0 1.7 fusion.21
  931.7 26.1 %subtract_bitcast_fusion = f32[8192,512]{0,1:T(8,128)} fusion(f32[512,8192]{1,0:T(8,128)} %convolution_subtract_fusion, f32[512,256]{1,0:T(8,128)S(1)} %fusion.21, f32[1,256,8192]{2,1,0:T(8,128)} %all-gather.15.cloned.1.call-done), kind=kOutput, calls=%fused_computation.1 | convolution fusion | flops 12889096192 | bytes 42467328 | tf_op jit(solution)/shard_map/dot_general | solution.py:12
  957.7 17.4 %copy.5 = f32[8192,512]{1,0:T(8,128)} copy(f32[8192,512]{0,1:T(8,128)} %subtract_bitcast_fusion) | data formatting | bytes 33554432 | tf_op jit(solution)/shard_map/sub | solution.py:30
Async XLA Ops:
  18.2 370.3 %all-to-all-start = ((f32[64,8,8192]{2,0,1:T(8,128)}), f32[64,8,8192]{2,0,1:T(8,128)}, u32[]{:S(2)}, u32[]{:S(2)}) async-start(f32[64,8,8192]{2,0,1:T(8,128)} %bitcast.65), calls=%async_computation | async-start | bytes 33554432 | tf_op jit(solution)/shard_map/all_to_all | solution.py:22
  25.5 66.8 %all-gather.9.cloned.1.call-start = ((), (), s32[]{:S(2)}) async-start(), calls=%async_computation.5 | async-start | bytes 10485760 | tf_op jit(solution)/shard_map/all_gather | solution.py:26
  32.4 447.1 %all-reduce.5.cloned.1.call-start = ((), (), s32[]{:S(2)}) async-start(), calls=%async_computation.1 | async-start | bytes 1048576 | tf_op jit(solution)/shard_map/psum | solution.py:28
  388.5 91.0 %copy-start = (f32[4,256,256]{2,1,0:T(8,128)S(1)}, f32[4,256,256]{2,1,0:T(8,128)}, u32[]{:S(2)}) copy-start(f32[4,256,256]{2,1,0:T(8,128)} %param.5) | copy-start | bytes 3145732
  408.0 130.8 %all-gather.11.cloned.1.call-start = ((), (), s32[]{:S(2)}) async-start(), calls=%async_computation.6 | async-start | bytes 10485760 | tf_op jit(solution)/shard_map/all_gather | solution.py:26
  408.7 221.0 %all-reduce.7.cloned.1.call-start = ((), (), s32[]{:S(2)}) async-start(), calls=%async_computation.2 | async-start | bytes 1048576 | tf_op jit(solution)/shard_map/psum | solution.py:28
  557.3 131.5 %all-gather.13.cloned.1.call-start = ((), (), s32[]{:S(2)}) async-start(), calls=%async_computation.7 | async-start | bytes 10485760 | tf_op jit(solution)/shard_map/all_gather | solution.py:26
  557.8 221.9 %all-reduce.9.cloned.1.call-start = ((), (), s32[]{:S(2)}) async-start(), calls=%async_computation.3 | async-start | bytes 1048576 | tf_op jit(solution)/shard_map/psum | solution.py:28
  707.3 131.8 %all-gather.15.cloned.1.call-start = ((), (), s32[]{:S(2)}) async-start(), calls=%async_computation.8 | async-start | bytes 10485760 | tf_op jit(solution)/shard_map/all_gather | solution.py:26
  708.0 222.0 %all-reduce.11.cloned.1.call-start = ((), (), s32[]{:S(2)}) async-start(), calls=%async_computation.4 | async-start | bytes 1048576 | tf_op jit(solution)/shard_map/psum | solution.py:28
Sparse Core Ops, SparseCore 0:
  32.6 59.6 all-gather.8
  408.1 71.3 all-reduce.4
  481.2 57.5 all-gather.10
  557.4 72.3 all-reduce.6
  631.2 57.5 all-gather.12
  707.4 72.3 all-reduce.8
  781.4 57.5 all-gather.14
  857.6 72.3 all-reduce.10
where the time goes:
time: 988 us; the launch traced here: 982 us
  waiting for transfers between devices  738 us (75%)
  matrix products  185 us (19%)
  local copies, waits for them, and re-layouts  36 us (4%)
  between operations  13.8 us (1%)
    all_to_all x1, waiting for transfers between devices, body(): lax.all_to_all(eigvecs, 'row', split_axis=1, concat_axis=0, tiled=True)  296 us
    psum x4, waiting for transfers between devices, body(): inner_sum = lax.psum(inner_part, 'row')  286 us
    all_gather x4, waiting for transfers between devices, body(): vectors = lax.all_gather(reflectors[block], 'col', axis=0, tiled=True)  154 us
    dot_general x4, matrix products, inner_rows(): lax.dot_general(left, right, (((0,), (0,)), ((), ())), precision=lax.Prec...  104 us
    dot_general x8, matrix products, matmul(): jnp.dot(left, right, precision=lax.Precision.HIGHEST, preferred_element_t...  81.7 us
  transfers between devices with their start and end apart: 9, of which 9 were waited for; matrix products, arithmetic and copies ran while one was open for 9% of the time, Pallas kernels for 0%

commit v1 on v0

--- a/solution.py
+++ b/solution.py
@@ -2,6 +2,28 @@
 import jax.numpy as jnp
 from jax import lax
 from jax.sharding import PartitionSpec as P
+
+
+def in_order(blocks, dim):
+    shape = list(blocks.shape[1:])
+    shape[dim] *= blocks.shape[0]
+    return jnp.moveaxis(blocks, 0, dim).reshape(shape)
+
+
+def collected_by_bits(value, axis):
+    count = lax.axis_size(axis)
+    tiles = value[None]
+    for level in range(count.bit_length() - 1):
+        stride = 1 << level
+        theirs = lax.ppermute(tiles, axis, [(i, i ^ stride) for i in range(count)])
+        both = jnp.stack([tiles, theirs])
+        upper = lax.axis_index(axis) >> level & 1
+        tiles = jnp.where(upper == 0, both, both[::-1]).reshape(-1, *value.shape)
+    return tiles
+
+
+def gather_by_bits(x, axis, dim):
+    return in_order(collected_by_bits(x, axis), dim)
 
 
 def matmul(left, right):
@@ -23,7 +45,7 @@
     current = arrived.T
     blocks = tfactors.shape[0]
     for block in range(blocks - 1, -1, -1):
-        vectors = lax.all_gather(reflectors[block], "col", axis=0, tiled=True)
+        vectors = gather_by_bits(reflectors[block], "col", 0)
         inner_part = matmul(vectors, current)
         inner_sum = lax.psum(inner_part, "row")
         scaled = matmul(tfactors[block], inner_sum)

time: 988 us -> 914 us (0.925)
  waiting for transfers between devices: 738 us -> 546 us
  other arithmetic: 0 us -> 70.4 us
  matrix products: 185 us -> 224 us
    ppermute x0 -> x8, waiting for transfers between devices: none -> 247 us  [collected_by_bits(): theirs = lax.ppermute(tiles, axis, [(i, i ^ stride) for i in range(count)])]
    all_to_all x1, waiting for transfers between devices: 296 us -> 57.8 us  [body(): lax.all_to_all(eigvecs, 'row', split_axis=1, concat_axis=0, tiled=True)]
    all_gather x4 -> x0, waiting for transfers between devices: 154 us -> none  [body(): vectors = lax.all_gather(reflectors[block], 'col', axis=0, tiled=True)]
    psum x4, waiting for transfers between devices: 286 us -> 241 us  [body(): inner_sum = lax.psum(inner_part, 'row')]
    another operation x0 -> x12, other arithmetic: none -> 41.8 us  [collected_by_bits(): both = jnp.stack([tiles, theirs])]
    dot_general x4, matrix products: 104 us -> 140 us  [inner_rows(): lax.dot_general(left, right, (((0,), (0,)), ((), ())), precision=lax.Prec...]
    select_n x0 -> x4, other arithmetic: none -> 28.6 us  [collected_by_bits(): tiles = jnp.where(upper == 0, both, both[::-1]).reshape(-1, *value.shape)]
    all_to_all x1 -> x2, local copies, waits for them, and re-layouts: 11.7 us -> 29.2 us  [body(): lax.all_to_all(eigvecs, 'row', split_axis=1, concat_axis=0, tiled=True)]
  transfers between devices with their start and end apart: 9 -> 13, of which waited for: 9 -> 9; matrix products, arithmetic and copies ran while one was open for 9% -> 19% of each run, Pallas kernels for 0% -> 0%
where the time goes in v1:
time: 914 us; the launch traced here: 907 us
  waiting for transfers between devices  546 us (60%)
  matrix products  224 us (25%)
  other arithmetic  70.4 us (8%)
  local copies, waits for them, and re-layouts  40.3 us (4%)
  between operations  13.7 us (1%)
  starting transfers between devices  12.6 us (1%)
    ppermute x8, waiting for transfers between devices, collected_by_bits(): theirs = lax.ppermute(tiles, axis, [(i, i ^ stride) for i in range(count)])  247 us
    psum x4, waiting for transfers between devices, body(): inner_sum = lax.psum(inner_part, 'row')  241 us
    dot_general x4, matrix products, inner_rows(): lax.dot_general(left, right, (((0,), (0,)), ((), ())), precision=lax.Prec...  140 us
    dot_general x8, matrix products, matmul(): jnp.dot(left, right, precision=lax.Precision.HIGHEST, preferred_element_t...  84.2 us
    all_to_all x1, waiting for transfers between devices, body(): lax.all_to_all(eigvecs, 'row', split_axis=1, concat_axis=0, tiled=True)  57.8 us
    another operation x12, other arithmetic, collected_by_bits(): both = jnp.stack([tiles, theirs])  41.8 us
    all_to_all x2, local copies, waits for them, and re-layouts, body(): lax.all_to_all(eigvecs, 'row', split_axis=1, concat_axis=0, tiled=True)  29.2 us
    select_n x4, other arithmetic, collected_by_bits(): tiles = jnp.where(upper == 0, both, both[::-1]).reshape(-1, *value.shape)  28.6 us
  transfers between devices with their start and end apart: 13, of which 9 were waited for; matrix products, arithmetic and copies ran while one was open for 19% of the time, Pallas kernels for 0%

profile of v1, /device:TPU:0, one launch (start us, length us, event | category | flops | bytes accessed | tf_op | source)
XLA Modules:
  0.0 907.0 jit_solution(8800807965265376131)
XLA Ops:
  6.5 11.7 %copy.28 = f32[8,8,8,8192]{3,2,0,1:T(8,128)} copy(f32[8,8,8,8192]{3,2,1,0:T(8,128)} %bitcast.100) | data formatting | bytes 33554432 | tf_op jit(solution)/shard_map/all_to_all | solution.py:44
  18.2 7.3 all-to-all-start
  25.5 0.0 all-reduce.5.cloned.1.call-start
  25.5 9.1 %slice_bitcast_fusion = (f32[1,1,64,8192]{3,2,0,1:T(8,128)}, f32[1,1,64,8192]{3,2,0,1:T(8,128)}, f32[1,1,64,8192]{3,2,1,0:T(8,128)S(1)}, f32[1,1,64,8192]{3,2,0,...) fusion(f32[4,64,8192]{2,1,0:T(8,128)} %param.4), kind=kLoop, calls=%fused_computation.41 | loop fusion | bytes 25165824 | tf_op jit(solution)/shard_map/stack;broadcast_in_dim;squeeze | solution.py:19
  34.6 0.0 collective-permute-start
  34.6 0.5 collective-permute-start.2
  35.1 0.0 collective-permute-start.4
  35.1 0.5 collective-permute-start.6
  35.6 3.5 collective-permute-done
  39.1 2.5 pad_maximum_fusion.4
  41.6 0.5 fusion.1
  42.2 1.6 collective-permute-start.1
  43.8 0.0 collective-permute-done.2
  43.8 1.9 pad_maximum_fusion.5
  45.7 0.0 copy-start.1
  45.7 2.6 fusion.3
  48.2 0.5 collective-permute-start.3
  48.8 0.0 collective-permute-done.4
  48.8 2.0 pad_maximum_fusion.6
  50.8 4.5 fusion.5
  55.3 1.5 collective-permute-start.5
  56.8 0.0 collective-permute-done.6
  56.8 2.0 pad_maximum_fusion.7
  58.8 4.5 fusion.7
  63.4 0.5 collective-permute-start.7
  63.9 71.8 %collective-permute-done.1 = f32[2,64,8192]{2,1,0:T(8,128)S(1)} collective-permute-done((f32[2,64,8192]{2,1,0:T(8,128)S(1)}, f32[2,64,8192]{2,1,0:T(8,128)S(1)}, u32[]{:S(2)}, u32[]{:S(2)}) %collective-permute-start.1) | collective-permute-done | bytes 4194336 | tf_op jit(solution)/shard_map/ppermute | solution.py:18
  135.7 2.0 copy-done.2
  137.7 3.0 pad_maximum_fusion
  140.7 85.0 %collective-permute-done.3 = f32[2,64,8192]{2,1,0:T(8,128)} collective-permute-done((f32[2,64,8192]{2,1,0:T(8,128)}, f32[2,64,8192]{2,1,0:T(8,128)}, u32[]{:S(2)}, u32[]{:S(2)}) %collective-permute-start.3) | collective-permute-done | bytes 4194336 | tf_op jit(solution)/shard_map/ppermute | solution.py:18
  225.6 3.0 pad_maximum_fusion.1
  228.7 86.9 %collective-permute-done.5 = f32[2,64,8192]{2,1,0:T(8,128)} collective-permute-done((f32[2,64,8192]{2,1,0:T(8,128)}, f32[2,64,8192]{2,1,0:T(8,128)}, u32[]{:S(2)}, u32[]{:S(2)}) %collective-permute-start.5) | collective-permute-done | bytes 4194336 | tf_op jit(solution)/shard_map/ppermute | solution.py:18
  315.5 7.6 pad_maximum_fusion.2
  323.1 3.9 reverse_select_fusion.3
  327.0 3.8 reverse_select_fusion.2
  330.8 57.8 %all-to-all-done = f32[64,8,8192]{2,0,1:T(8,128)} async-done(((f32[64,8,8192]{2,0,1:T(8,128)}), f32[64,8,8192]{2,0,1:T(8,128)}, u32[]{:S(2)}, u32[]{:S(2)}) %all-to-all-start) | async-done | bytes 16777248 | tf_op jit(solution)/shard_map/all_to_all | solution.py:44
  388.6 19.6 %fusion.20 = f32[256,512]{1,0:T(8,128)} fusion(f32[256,8192]{1,0:T(8,128)} %bitcast.93, f32[512,8192]{1,0:T(8,128)} %bitcast.1), kind=kOutput, calls=%fused_computation.45 | convolution fusion | flops 12884901888 | bytes 25690112 | tf_op jit(solution)/shard_map/dot_general | solution.py:30
  408.2 0.0 all-reduce.5.cloned.1.call-update
  408.2 0.0 all-reduce.7.cloned.1.call-start
  408.2 10.5 %reverse_select_fusion.1 = f32[2,2,64,8192]{3,2,1,0:T(8,128)} fusion(f32[2,2,64,8192]{3,2,1,0:T(8,128)} %pad_maximum_fusion.2, pred[]{:T(512)S(6)} %eq.4), kind=kLoop, calls=%fused_computation.3 | loop fusion | flops 2097152 | bytes 16777216 | tf_op jit(solution)/shard_map/jit(_where)/select_n | solution.py:21
  418.7 17.6 %copy.21 = f32[512,8192]{0,1:T(8,128)} copy(f32[512,8192]{1,0:T(8,128)} %bitcast.1) | data formatting | bytes 33554432 | tf_op jit(solution)/shard_map/all_to_all | solution.py:44
  436.3 43.4 %all-reduce.5.cloned.1.call-done = f32[256,512]{1,0:T(8,128)} async-done(((f32[256,512]{1,0:T(8,128)}), f32[256,512]{1,0:T(8,128)}) %all-reduce.5.cloned.1.call-update) | async-done | bytes 524304 | tf_op jit(solution)/shard_map/psum | solution.py:50
  479.7 2.0 fusion.14
  481.7 35.3 %bitcast_subtract_fusion = f32[8192,512]{1,0:T(8,128)} fusion(f32[512,8192]{0,1:T(8,128)} %copy.21, f32[256,8192]{1,0:T(8,128)} %bitcast.94, f32[512,256]{1,0:T(8,128)S(1)} %fusion.14), kind=kOutput, calls=%fused_computation.1 | convolution fusion | flops 12889096192 | bytes 42467328 | tf_op jit(solution)/shard_map/dot_general | solution.py:34
  517.0 19.4 %fusion.21 = f32[256,512]{1,0:T(8,128)} fusion(f32[256,8192]{1,0:T(8,128)} %bitcast.91, f32[8192,512]{1,0:T(8,128)} %bitcast_subtract_fusion), kind=kOutput, calls=%fused_computation.46 | convolution fusion | flops 12884901888 | bytes 25690112 | tf_op jit(solution)/shard_map/dot_general | solution.py:30
  536.4 0.0 all-reduce.7.cloned.1.call-update
  536.4 0.0 all-reduce.9.cloned.1.call-start
  536.5 0.0 collective-permute-done.7
  536.5 7.6 pad_maximum_fusion.3
  544.1 64.1 %all-reduce.7.cloned.1.call-done = f32[256,512]{1,0:T(8,128)} async-done(((f32[256,512]{1,0:T(8,128)}), f32[256,512]{1,0:T(8,128)}) %all-reduce.7.cloned.1.call-update) | async-done | bytes 524304 | tf_op jit(solution)/shard_map/psum | solution.py:50
  608.2 2.0 fusion.12
  610.3 35.1 %convolution_subtract_fusion.2 = f32[8192,512]{1,0:T(8,128)} fusion(f32[8192,512]{1,0:T(8,128)} %bitcast_subtract_fusion, f32[256,8192]{1,0:T(8,128)} %bitcast.92, f32[512,256]{1,0:T(8,128)S(1)} %fusion.12), kind=kOutput, calls=%fused_computation.8 | convolution fusion | flops 12889096192 | bytes 42467328 | tf_op jit(solution)/shard_map/dot_general | solution.py:34
  645.3 19.4 %fusion.22 = f32[256,512]{1,0:T(8,128)} fusion(f32[256,8192]{1,0:T(8,128)} %bitcast.89, f32[8192,512]{1,0:T(8,128)} %convolution_subtract_fusion.2), kind=kOutput, calls=%fused_computation.47 | convolution fusion | flops 12884901888 | bytes 25690112 | tf_op jit(solution)/shard_map/dot_general | solution.py:30
  664.7 0.0 all-reduce.9.cloned.1.call-update
  664.7 0.0 all-reduce.11.cloned.1.call-start
  664.8 10.4 %reverse_select_fusion = f32[2,2,64,8192]{3,2,1,0:T(8,128)} fusion(f32[2,2,64,8192]{3,2,1,0:T(8,128)} %pad_maximum_fusion.3, pred[]{:T(512)S(6)} %eq.4), kind=kLoop, calls=%fused_computation.2 | loop fusion | flops 2097152 | bytes 16777216 | tf_op jit(solution)/shard_map/jit(_where)/select_n | solution.py:21
  675.2 61.3 %all-reduce.9.cloned.1.call-done = f32[256,512]{1,0:T(8,128)} async-done(((f32[256,512]{1,0:T(8,128)}), f32[256,512]{1,0:T(8,128)}) %all-reduce.9.cloned.1.call-update) | async-done | bytes 524304 | tf_op jit(solution)/shard_map/psum | solution.py:50
  736.6 2.2 fusion.10
  738.7 0.0 slice-start.1
  738.8 35.2 %convolution_subtract_fusion.1 = f32[8192,512]{1,0:T(8,128)} fusion(f32[8192,512]{1,0:T(8,128)} %convolution_subtract_fusion.2, f32[256,8192]{1,0:T(8,128)} %bitcast.90, f32[512,256]{1,0:T(8,128)S(1)} %fusion.10), kind=kOutput, calls=%fused_computation.7 | convolution fusion | flops 12889096192 | bytes 42467328 | tf_op jit(solution)/shard_map/dot_general | solution.py:34
  774.0 17.6 %fusion.23 = f32[256,512]{1,0:T(8,128)} fusion(f32[256,8192]{1,0:T(8,128)S(1)} %bitcast.98, f32[8192,512]{1,0:T(8,128)} %convolution_subtract_fusion.1), kind=kOutput, calls=%fused_computation.48 | convolution fusion | flops 12884901888 | bytes 25690112 | tf_op jit(solution)/shard_map/dot_general | solution.py:30
  791.5 0.0 all-reduce.11.cloned.1.call-update
  791.6 71.7 %all-reduce.11.cloned.1.call-done = f32[256,512]{1,0:T(8,128)} async-done(((f32[256,512]{1,0:T(8,128)}), f32[256,512]{1,0:T(8,128)}) %all-reduce.11.cloned.1.call-update) | async-done | bytes 524304 | tf_op jit(solution)/shard_map/psum | solution.py:50
  863.3 2.1 fusion.8
  865.4 34.7 %convolution_subtract_fusion = f32[8192,512]{1,0:T(8,128)} fusion(f32[8192,512]{1,0:T(8,128)} %convolution_subtract_fusion.1, f32[256,8192]{1,0:T(8,128)} %bitcast.95, f32[512,256]{1,0:T(8,128)S(1)} %fusion.8), kind=kOutput, calls=%fused_computation.6 | convolution fusion | flops 12889096192 | bytes 42467328 | tf_op jit(solution)/shard_map/dot_general | solution.py:34
  (10 shorter events, 0.0 us)
Async XLA Ops:
  18.2 370.4 %all-to-all-start = ((f32[64,8,8192]{2,0,1:T(8,128)}), f32[64,8,8192]{2,0,1:T(8,128)}, u32[]{:S(2)}, u32[]{:S(2)}) async-start(f32[64,8,8192]{2,0,1:T(8,128)} %bitcast.99), calls=%async_computation | async-start | bytes 33554432 | tf_op jit(solution)/shard_map/all_to_all | solution.py:44
  25.5 454.2 %all-reduce.5.cloned.1.call-start = ((), (), s32[]{:S(2)}) async-start(), calls=%async_computation.1 | async-start | bytes 1048576 | tf_op jit(solution)/shard_map/psum | solution.py:50
  34.6 4.5 collective-permute-start
  34.6 9.2 %collective-permute-start.2 = (f32[1,64,8192]{2,1,0:T(8,128)}, f32[1,64,8192]{2,1,0:T(8,128)}, u32[]{:S(2)}, u32[]{:S(2)}) collective-permute-start(f32[1,64,8192]{2,1,0:T(8,128)} %get-tuple-element.9), channel_id=1, source_target_pairs={{0,1},{1,0},{2,3},{3,2},{4,5},{5,4},{6,7},{7,6},{8,9},{9,8},{10,11... | collective-permute-start | bytes 6291464 | tf_op jit(solution)/shard_map/ppermute | solution.py:18
  35.1 13.6 %collective-permute-start.4 = (f32[1,64,8192]{2,1,0:T(8,128)}, f32[1,64,8192]{2,1,0:T(8,128)}, u32[]{:S(2)}, u32[]{:S(2)}) collective-permute-start(f32[1,64,8192]{2,1,0:T(8,128)} %get-tuple-element.12), channel_id=1, source_target_pairs={{0,1},{1,0},{2,3},{3,2},{4,5},{5,4},{6,7},{7,6},{8,9},{9,8},{10,11... | collective-permute-start | bytes 6291464 | tf_op jit(solution)/shard_map/ppermute | solution.py:18
  35.1 21.7 %collective-permute-start.6 = (f32[1,64,8192]{2,1,0:T(8,128)}, f32[1,64,8192]{2,1,0:T(8,128)}, u32[]{:S(2)}, u32[]{:S(2)}) collective-permute-start(f32[1,64,8192]{2,1,0:T(8,128)} %get-tuple-element.11), channel_id=1, source_target_pairs={{0,1},{1,0},{2,3},{3,2},{4,5},{5,4},{6,7},{7,6},{8,9},{9,8},{10,11... | collective-permute-start | bytes 6291464 | tf_op jit(solution)/shard_map/ppermute | solution.py:18
  42.2 93.5 %collective-permute-start.1 = (f32[2,64,8192]{2,1,0:T(8,128)S(1)}, f32[2,64,8192]{2,1,0:T(8,128)S(1)}, u32[]{:S(2)}, u32[]{:S(2)}) collective-permute-start(f32[2,64,8192]{2,1,0:T(8,128)S(1)} %get-tuple-element.20), channel_id=1, source_target_pairs={{0,2},{1,3},{2,0},{3,1},{4,6},{5,7},{6,4},{7,5},{8,10},{9,11},{10,... | collective-permute-start | bytes 12582920 | tf_op jit(solution)/shard_map/ppermute | solution.py:18
  45.7 3.1 copy-start.1
  48.2 177.4 %collective-permute-start.3 = (f32[2,64,8192]{2,1,0:T(8,128)}, f32[2,64,8192]{2,1,0:T(8,128)}, u32[]{:S(2)}, u32[]{:S(2)}) collective-permute-start(f32[2,64,8192]{2,1,0:T(8,128)} %get-tuple-element.18), channel_id=1, source_target_pairs={{0,2},{1,3},{2,0},{3,1},{4,6},{5,7},{6,4},{7,5},{8,10},{9,11},{10,... | collective-permute-start | bytes 12582920 | tf_op jit(solution)/shard_map/ppermute | solution.py:18
  50.8 6.1 copy-start
  55.3 260.2 %collective-permute-start.5 = (f32[2,64,8192]{2,1,0:T(8,128)}, f32[2,64,8192]{2,1,0:T(8,128)}, u32[]{:S(2)}, u32[]{:S(2)}) collective-permute-start(f32[2,64,8192]{2,1,0:T(8,128)} %get-tuple-element.16), channel_id=1, source_target_pairs={{0,2},{1,3},{2,0},{3,1},{4,6},{5,7},{6,4},{7,5},{8,10},{9,11},{10,... | collective-permute-start | bytes 12582920 | tf_op jit(solution)/shard_map/ppermute | solution.py:18
  63.4 473.1 %collective-permute-start.7 = (f32[2,64,8192]{2,1,0:T(8,128)}, f32[2,64,8192]{2,1,0:T(8,128)}, u32[]{:S(2)}, u32[]{:S(2)}) collective-permute-start(f32[2,64,8192]{2,1,0:T(8,128)} %get-tuple-element.14), channel_id=1, source_target_pairs={{0,2},{1,3},{2,0},{3,1},{4,6},{5,7},{6,4},{7,5},{8,10},{9,11},{10,... | collective-permute-start | bytes 12582920 | tf_op jit(solution)/shard_map/ppermute | solution.py:18
  135.7 2.0 copy-start.2
  408.2 200.1 %all-reduce.7.cloned.1.call-start = ((), (), s32[]{:S(2)}) async-start(), calls=%async_computation.2 | async-start | bytes 1048576 | tf_op jit(solution)/shard_map/psum | solution.py:50
  418.7 61.0 %copy-start.3 = (f32[4,256,256]{2,1,0:T(8,128)S(1)}, f32[4,256,256]{2,1,0:T(8,128)}, u32[]{:S(2)}) copy-start(f32[4,256,256]{2,1,0:T(8,128)} %param.5) | copy-start | bytes 3145732
  536.4 200.1 %all-reduce.9.cloned.1.call-start = ((), (), s32[]{:S(2)}) async-start(), calls=%async_computation.3 | async-start | bytes 1048576 | tf_op jit(solution)/shard_map/psum | solution.py:50
  664.7 198.6 %all-reduce.11.cloned.1.call-start = ((), (), s32[]{:S(2)}) async-start(), calls=%async_computation.4 | async-start | bytes 1048576 | tf_op jit(solution)/shard_map/psum | solution.py:50
  736.5 37.4 %slice-start = ((s8[8388608]{0:T(1024)(128)(4,1)}), s8[4194304]{0:T(1024)(128)(4,1)S(1)}, s32[]{:S(2)}) async-start(s8[8388608]{0:T(1024)(128)(4,1)} %bitcast.96), calls=%async_computation.5 | async-start | bytes 8388608
  738.7 35.2 %slice-start.1 = ((s8[8388608]{0:T(1024)(128)(4,1)}), s8[4194304]{0:T(1024)(128)(4,1)S(1)}, s32[]{:S(2)}) async-start(s8[8388608]{0:T(1024)(128)(4,1)} %bitcast.96), calls=%async_computation.6 | async-start | bytes 8388608
Sparse Core Ops, SparseCore 0:
  408.3 71.3 all-reduce.4
  536.5 71.6 all-reduce.6
  664.9 71.6 all-reduce.8
  791.7 71.5 all-reduce.10
